TPU v7x, 256 devices: a whole 4x4x8 slice. The times are simulated.
256 devices in a mesh: src: 64 (over x, z, core), tgt: 4 (over y).
Axes of the slice: x: 4, y: 4, z: 8, core: 2. Of those that a mesh axis runs over, the one named last changes fastest.
Arguments:
- source: bfloat16 [65536, 300], P('src'), may hold values from -8 to 8
- target: bfloat16 [8192, 300], P(('tgt', 'src')), may hold values from -8 to 8
- rotation: bfloat16 [300, 300], replicated, may hold values from -0.5 to 1.5
Outputs:
- src_potential: float32 [65536], P('src')
- tgt_potential: float32 [8192], P('tgt')
- matched: float32 [65536, 300], P('src', 'tgt')
- rotation_grad: float32 [300, 300], replicated
All inputs are finite; a program needn't handle non-finite values.
Results may differ from a plain program's by a relative error of at most 0.0003.
The roundings to bfloat16 on the way count: a program that leaves them out, or rounds other values in their place, can miss the bound.
Values may be sent and summed in bfloat16 or wider, within the bound.
A program may use at most 64 MiB of HBM per device.

v0:
```python
import math

import jax
import jax.numpy as jnp
from jax import lax
from jax.sharding import PartitionSpec as P

SWEEPS = 2


epsilon = 2.0


def shards(source, target, rotation):
    width = source.shape[1]
    row_count = source.shape[0]
    targets_all = lax.all_gather(target, "src", axis=0, tiled=True)
    rotated = jnp.dot(targets_all, rotation.T, preferred_element_type=jnp.float32).astype(
        jnp.bfloat16
    )
    col_count = targets_all.shape[0]
    total_rows = row_count * lax.axis_size("src")
    total_cols = col_count * lax.axis_size("tgt")
    block = math.gcd(col_count, 512)
    nblocks = col_count // block
    rotated_blocks = rotated.reshape(nblocks, block, width)
    target_blocks = targets_all.reshape(nblocks, block, width)
    inv_root = 1.0 / math.sqrt(width)

    def cost_block(piece):
        return (
            -jnp.einsum("rd,cd->rc", source, piece, preferred_element_type=jnp.float32) * inv_root
        )

    src_pot = jnp.zeros((row_count,), jnp.float32)
    tgt_pot = jnp.zeros((col_count,), jnp.float32)
    for sweep in range(SWEEPS):

        def one_block(piece):
            scaled = (src_pot[:, None] - cost_block(piece)) / epsilon
            top = jnp.max(scaled, axis=0)
            return (top, jnp.sum(jnp.exp(scaled - top[None, :]), axis=0))

        tops, totals = lax.map(one_block, rotated_blocks)
        tops, totals = (tops.reshape(col_count), totals.reshape(col_count))
        peak = lax.pmax(tops, "src")
        totals = lax.psum(totals * jnp.exp(tops - peak), "src")
        tops = peak
        tgt_pot = epsilon * math.log(total_rows) - epsilon * (tops + jnp.log(totals))
        pot_blocks = tgt_pot.reshape(nblocks, block)

        def row_step(carry, pieces):
            top, total = carry
            piece, pot = pieces
            scaled = (pot[None, :] - cost_block(piece)) / epsilon
            new_top = jnp.maximum(top, jnp.max(scaled, axis=1))
            total = total * jnp.exp(top - new_top) + jnp.sum(
                jnp.exp(scaled - new_top[:, None]), axis=1
            )
            return ((new_top, total), None)

        start = (
            jnp.full((row_count,), -jnp.inf, jnp.float32),
            jnp.zeros((row_count,), jnp.float32),
        )
        result, row_unused = lax.scan(row_step, start, (rotated_blocks, pot_blocks))
        row_tops, row_totals = result
        row_peak = lax.pmax(row_tops, "tgt")
        row_totals = lax.psum(row_totals * jnp.exp(row_tops - row_peak), "tgt")
        row_tops = row_peak
        src_pot = epsilon * math.log(total_cols) - epsilon * (row_tops + jnp.log(row_totals))
    final_blocks = tgt_pot.reshape(nblocks, block)

    def plan_step(accum, pieces):
        piece, pot, vectors = pieces
        weights = jnp.exp((src_pot[:, None] + pot[None, :] - cost_block(piece)) / epsilon).astype(
            jnp.bfloat16
        )
        return (accum + jnp.dot(weights, vectors, preferred_element_type=jnp.float32), None)

    accum, unused = lax.scan(
        plan_step,
        jnp.zeros((row_count, width), jnp.float32),
        (rotated_blocks, final_blocks, target_blocks),
    )
    factor = epsilon * math.sqrt(width) / total_rows
    source_wide = source.astype(jnp.float32)
    full_rows = lax.psum(accum, "tgt") / total_cols
    share = width // lax.axis_size("tgt")
    matched = lax.dynamic_slice_in_dim(full_rows, lax.axis_index("tgt") * share, share, 1)
    partial_grad = jnp.dot(source_wide.T, full_rows, precision=lax.Precision.HIGHEST) * factor
    rotation_grad = lax.psum(partial_grad, "src")
    return (src_pot, tgt_pot, matched, rotation_grad)


def solution(mesh):
    placed = (P("src", None), P(("tgt", "src"), None), P())
    return jax.shard_map(
        shards,
        mesh=mesh,
        in_specs=placed,
        out_specs=(P("src"), P("tgt"), P("src", "tgt"), P()),
        check_vma=False,
    )
```

profile of v0, /device:TPU:1, one launch (start us, length us, event | category | flops | bytes accessed | tf_op | source)
XLA Modules:
  0.0 927.7 jit_solution(1813642293154081171)
XLA Ops:
  7.2 0.7 all-gather.2.cloned.1.call-update
  8.0 83.9 %all-gather.2.cloned.1.call-done = bf16[2048,300]{1,0:T(8,128)(2,1)} async-done(((bf16[32,300]{1,0:T(8,128)(2,1)}), bf16[2048,300]{1,0:T(8,128)(2,1)}) %all-gather.2.cloned.1.call-update) | async-done | bytes 1228816 | tf_op jit(solution)/shard_map/all_gather | solution.py:17
  91.9 2.2 convolution_convert_fusion
  94.2 1.6 copy.13
  95.7 9.6 %while.61 = (s32[]{:T(128)}, f32[4,512]{1,0:T(4,128)S(1)}, f32[4,512]{1,0:T(4,128)S(1)}, bf16[4,512,300]{2,1,0:T(8,128)(2,1)}, bf16[1024,300]{0,1:T(8,128)(2,1)S(1)}, /*index=5*/s32[]{:T(128)}, s32[]{:T(128)}) while((s32[]{:T(128)}, f32[4,512]{1,0:T(4,128)S(1)}, f32[4,512]{1,0:T(4,128)S(1)}, bf16[4,512,300]{2,1,0:T(8,128)(2,1)}, ...), condition=%wide.region_3.4_spmd, body=%wide.region_0.3_spmd.sunk | while | flops 318241792 | bytes 5216853 | solution.py:44
  95.8 1.8 fusion.58
  97.6 0.5 exponential_reduce_fusion.8
  98.2 1.8 fusion.58
  100.0 0.5 exponential_reduce_fusion.8
  100.6 1.8 fusion.58
  102.4 0.5 exponential_reduce_fusion.8
  103.0 1.8 fusion.58
  104.8 0.5 exponential_reduce_fusion.8
  105.4 125.6 %pmax.28 = f32[2048]{0:T(1024)S(1)} all-reduce(f32[2048]{0:T(1024)S(1)} %bitcast.107), channel_id=1, replica_groups=mesh['src'=64,'tgt'=4] {'src'}, use_global_device_ids=true, to_apply=%region_4.5 | all-reduce | flops 2048 | bytes 16384 | tf_op jit(solution)/shard_map/pmax | solution.py:46
  231.1 128.6 %psum.42 = f32[2048]{0:T(1024)S(1)} all-reduce(f32[2048]{0:T(1024)S(1)} %exponential_multiply_fusion.1), channel_id=1, replica_groups=mesh['src'=64,'tgt'=4] {'src'}, use_global_device_ids=true, to_apply=%region_5.6 | all-reduce | flops 2048 | bytes 16384 | tf_op jit(solution)/shard_map/psum | solution.py:47
  359.7 8.6 while.63
  359.7 1.7 fusion.62
  361.5 0.3 exponential_reduce_fusion.10
  361.9 1.7 fusion.62
  363.6 0.3 exponential_reduce_fusion.10
  364.0 1.7 fusion.62
  365.8 0.3 exponential_reduce_fusion.10
  366.2 1.7 fusion.62
  367.9 0.3 exponential_reduce_fusion.10
  368.3 8.5 pmax.29
  376.8 6.0 psum.43
  382.8 9.6 %while.62 = (s32[]{:T(128)}, f32[4,512]{1,0:T(4,128)S(1)}, f32[4,512]{1,0:T(4,128)S(1)}, f32[1024]{0:T(1024)S(1)}, bf16[4,512,300]{2,1,0:T(8,128)(2,1)}, /*index...) while((s32[]{:T(128)}, f32[4,512]{1,0:T(4,128)S(1)}, f32[4,512]{1,0:T(4,128)S(1)}, f32[1024]{0:T(1024)S(1)}, ...), condition=%wide.region_15.16_spmd, body=%wide.region_12.15_spmd.sunk | while | flops 318241792 | bytes 5220957 | solution.py:44
  382.8 1.8 fusion.60
  384.6 0.5 exponential_reduce_fusion.9
  385.1 0.1 dynamic_update_slice.19
  385.2 1.8 fusion.60
  387.0 0.5 exponential_reduce_fusion.9
  387.5 0.1 dynamic_update_slice.19
  387.6 1.8 fusion.60
  389.4 0.5 exponential_reduce_fusion.9
  389.9 0.1 dynamic_update_slice.19
  390.0 1.8 fusion.60
  391.8 0.5 exponential_reduce_fusion.9
  392.3 0.1 dynamic_update_slice.19
  392.4 129.9 %pmax.30 = f32[2048]{0:T(1024)S(1)} all-reduce(f32[2048]{0:T(1024)S(1)} %bitcast.109), channel_id=1, replica_groups=mesh['src'=64,'tgt'=4] {'src'}, use_global_device_ids=true, to_apply=%region_16.17 | all-reduce | flops 2048 | bytes 16384 | tf_op jit(solution)/shard_map/pmax | solution.py:46
  522.3 126.1 %psum.44 = f32[2048]{0:T(1024)S(1)} all-reduce(f32[2048]{0:T(1024)S(1)} %exponential_multiply_fusion), channel_id=1, replica_groups=mesh['src'=64,'tgt'=4] {'src'}, use_global_device_ids=true, to_apply=%region_17.18 | all-reduce | flops 2048 | bytes 16384 | tf_op jit(solution)/shard_map/psum | solution.py:47
  648.4 0.6 copy-done.3
  649.0 8.5 while.64
  649.0 1.7 fusion.65
  650.8 0.3 exponential_reduce_fusion.11
  651.2 1.7 fusion.65
  652.9 0.3 exponential_reduce_fusion.11
  653.3 1.7 fusion.65
  655.1 0.3 exponential_reduce_fusion.11
  655.4 1.7 fusion.65
  657.2 0.3 exponential_reduce_fusion.11
  657.6 7.7 pmax.31
  665.3 6.0 psum.45
  671.3 15.3 %while.65 = (s32[]{:T(128)}, f32[1024,300]{0,1:T(8,128)}, f32[1024]{0:T(1024)S(1)}, f32[4,512]{1,0:T(4,128)S(1)}, bf16[4,512,300]{2,1,0:T(8,128)(2,1)}, /*index=...) while((s32[]{:T(128)}, f32[1024,300]{0,1:T(8,128)}, ...), condition=%wide.region_25.26_spmd.clone, body=%wide.region_24.25_spmd.clone.sunk | while | flops 632905728 | bytes 3886187 | solution.py:81
  671.4 3.5 convolution_add_fusion.2
  674.9 3.9 convolution_add_fusion.2
  678.8 3.9 convolution_add_fusion.2
  682.7 3.9 convolution_add_fusion.2
  686.7 47.8 %all-reduce.3.cloned.1.call-done = f32[1024,300]{0,1:T(8,128)} async-done(((f32[1024,300]{0,1:T(8,128)}), f32[1024,300]{0,1:T(8,128)}) %all-reduce.3.cloned.1.call-update) | async-done | bytes 1228816 | tf_op jit(solution)/shard_map/psum | solution.py:88
  734.6 3.3 fusion.31
  737.9 0.1 broadcast_multiply_fusion
  738.1 0.8 constant_dynamic-slice_fusion.3
  738.8 180.3 %all-reduce.5.cloned.1.call-done = f32[300,300]{0,1:T(8,128)} async-done(((f32[300,300]{0,1:T(8,128)}), f32[300,300]{0,1:T(8,128)}) %all-reduce.5.cloned.1.call-update) | async-done | bytes 360016 | tf_op jit(solution)/shard_map/psum | solution.py:92
  919.2 2.0 copy.12
  (85 shorter events, 1.1 us)
Async XLA Ops:
  7.2 84.7 %copy-start = (bf16[300,300]{1,0:T(8,128)(2,1)S(1)}, bf16[300,300]{1,0:T(8,128)(2,1)}, u32[]{:S(2)}) copy-start(bf16[300,300]{1,0:T(8,128)(2,1)} %param.15) | copy-start | bytes 540004
  7.2 84.7 %all-gather.2.cloned.1.call-start = ((), (), s32[]{:S(2)}) async-start(), calls=%async_computation | async-start | bytes 1597440 | tf_op jit(solution)/shard_map/all_gather | solution.py:17
  7.9 726.7 %all-reduce.3.cloned.1.call-start = ((), (), s32[]{:S(2)}) async-start(), calls=%async_computation.1 | async-start | bytes 2490368 | tf_op jit(solution)/shard_map/psum | solution.py:88
  94.2 1.6 copy-start.2
  648.4 0.6 copy-start.3
  686.7 51.4 %copy-start.4 = (f32[1024]{0:T(1024)}, f32[1024]{0:T(1024)S(1)}, u32[]{:S(2)}) copy-start(f32[1024]{0:T(1024)S(1)} %get-tuple-element.684) | copy-start | bytes 12292
  686.7 232.5 %all-reduce.5.cloned.1.call-start = ((), (), s32[]{:S(2)}) async-start(), calls=%async_computation.2 | async-start | bytes 933888 | tf_op jit(solution)/shard_map/psum | solution.py:92
  734.6 3.3 copy-start.1
Sparse Core Ops, SparseCore 0:
  10.8 81.0 all-gather.1
  686.8 47.7 all-reduce.2
  739.0 180.0 all-reduce.4
where the time goes:
time: 929 us; the launch traced here: 928 us
  blocking collectives  538 us (58%)
  waiting for transfers between devices  313 us (34%)
  matrix products  49.1 us (5%)
  between operations  14 us (2%)
    pmax x2, blocking collectives, shards(): peak = lax.pmax(tops, 'src')  256 us
    psum x2, blocking collectives, shards(): totals = lax.psum(totals * jnp.exp(tops - peak), 'src')  255 us
    psum x1, waiting for transfers between devices, shards(): rotation_grad = lax.psum(partial_grad, 'src')  180 us
    all_gather x1, waiting for transfers between devices, shards(): targets_all = lax.all_gather(target, 'src', axis=0, tiled=True)  83.9 us
    psum x1, waiting for transfers between devices, shards(): full_rows = lax.psum(accum, 'tgt') / total_cols  47.8 us
    dot_general x16, matrix products, cost_block(): jnp.einsum('rd,cd->rc', source, piece, preferred_element_type=jnp.float32)  28.2 us
  transfers between devices with their start and end apart: 3, of which 3 were waited for; matrix products, arithmetic and copies ran while one was open for 0% of the time, Pallas kernels for 0%

commit v1 on v0

v1 whole, which is shorter than its diff:
```python
import functools
import math

import jax
import jax.numpy as jnp
from jax import lax
from jax.experimental import pallas as pl
from jax.experimental.pallas import tpu as pltpu
from jax.sharding import PartitionSpec as P

MESH = pl.DeviceIdType.MESH
F32 = jnp.float32
BF16 = jnp.bfloat16

XS, ZS, YS = 4, 8, 4
CHIPS = XS * ZS
D = 300
ROWS = 1024
COLS = 2048
NS, NT = 65536, 8192
EPS = 2.0
LN2 = math.log(2.0)
SLAB = 80
WIDE = YS * SLAB
CHUNK = 512
TILES = 64
NTD = (((1,), (1,)), ((), ()))
NND = (((1,), (0,)), ((), ()))


def dot(a, b, dims):
    return lax.dot_general(a, b, dims, preferred_element_type=F32)


def kernel(
    src_ref, tgt_ref, rot_ref,
    f_ref, g_ref, m_ref, grad_ref,
    G, R, GT, S, W, MT, RM, TOPB, RB,
    CV, CP, CX, CR, CF, GV,
    RV, RR, FV,
    GP, GB, GC, GS, GR, GO, GY, GZ, GF,
    gather_send, gather_recv, fwd_send, core_send,
    cp_send, cp_recv, cx_send, cx_recv, cf_send, cf_recv,
    rr_send, rr_recv, rm_send, rm_recv,
    gc_send, gc_recv, gr_send, gr_recv, gy_send, gy_recv, gz_send, gz_recv, gf_send, gf_recv,
):
    s = lax.axis_index("src")
    y = lax.axis_index("tgt")
    idx = s // 2
    c = s % 2
    x = idx // ZS
    z = idx % ZS
    mate = {"src": idx * 2 + (1 - c)}

    def chip(p):
        return {"src": p * 2 + c}

    def copy(a, b, ss, rs, to):
        return pltpu.make_async_remote_copy(
            src_ref=a, dst_ref=b, send_sem=ss, recv_sem=rs, device_id=to, device_id_type=MESH
        )

    barrier = pltpu.get_barrier_semaphore()

    @pl.loop(1, CHIPS)
    def _(d):
        pl.semaphore_signal(barrier, inc=1, device_id=chip((idx + d) % CHIPS), device_id_type=MESH)

    pl.semaphore_signal(barrier, inc=1, device_id=mate, device_id_type=MESH)
    for d in range(1, YS):
        pl.semaphore_signal(barrier, inc=1, device_id={"tgt": (y + d) % YS}, device_id_type=MESH)
    pl.semaphore_wait(barrier, CHIPS - 1 + 1 + YS - 1)

    def z_copy(d):
        return copy(
            tgt_ref, G.at[idx, c], gather_send.at[d], gather_recv.at[idx, c],
            chip(x * ZS + (z + d) % ZS),
        )

    def x_copy(p, d, k):
        return copy(
            G.at[p, c], G.at[p, c], fwd_send.at[d, k], gather_recv.at[p, c],
            chip(((x + d) % XS) * ZS + z),
        )

    def core_copy(xc, k):
        block = G.at[pl.ds(xc * ZS, ZS), c]
        return copy(block, block, core_send.at[k], gather_recv.at[xc * ZS, c], mate)

    def core_wait(xc, k):
        block = G.at[pl.ds(xc * ZS, ZS), 1 - c]
        copy(block, block, core_send.at[k], gather_recv.at[xc * ZS, 1 - c], mate).wait_recv()

    def arrived(p):
        copy(
            tgt_ref, G.at[p, c], gather_send.at[0], gather_recv.at[p, c], mate
        ).wait_recv()

    z_order = (1, 7, 2, 6, 3, 5, 4)
    x_order = (1, 3, 2)
    for d in z_order:
        z_copy(d).start()
    G[idx, c] = tgt_ref[...]
    for d in x_order:
        x_copy(idx, d, 0).start()
    for d in z_order:
        p = x * ZS + (z + d) % ZS
        arrived(p)
        for e in x_order:
            x_copy(p, e, d).start()
    core_copy(x, 0).start()

    a = lax.broadcasted_iota(jnp.int32, (WIDE, D), 0)
    b = lax.broadcasted_iota(jnp.int32, (WIDE, D), 1)
    hit = jnp.zeros((WIDE, D), jnp.bool_)
    for q in range(YS):
        hit = hit | ((a - SLAB * q == b - 75 * q) & (b >= 75 * q) & (b < 75 * q + 75))
    spread = jnp.where(hit, 1.0, 0.0).astype(BF16)

    scale = math.log2(math.e) / (EPS * math.sqrt(D))
    HALF = 256

    def chunk_work(xc):
        cols = pl.ds(pl.multiple_of(xc * CHUNK, CHUNK), CHUNK)
        words = G[pl.ds(xc * ZS, ZS)].reshape(CHUNK, D)
        GT[:, cols] = dot(spread, words, NTD).astype(BF16)
        R[...] = dot(words, rot_ref[...], NTD).astype(BF16)

        def fill(i, top):
            rows = pl.ds(pl.multiple_of(i * HALF, HALF), HALF)
            part = dot(src_ref[rows, :], R[...], NTD) * scale
            S[rows, cols] = part
            return jnp.maximum(top, jnp.max(part.reshape(HALF // 8, 8, CHUNK), axis=0))

        top = lax.fori_loop(0, ROWS // HALF, fill, jnp.full((8, CHUNK), -jnp.inf, F32))
        top = jnp.max(top, axis=0, keepdims=True)

        def add(i, total):
            rows = pl.ds(pl.multiple_of(i * 64, 64), 64)
            e = jnp.exp2(S[rows, cols] - top)
            return total + jnp.sum(e.reshape(8, 8, CHUNK), axis=0)

        total = lax.fori_loop(0, ROWS // 64, add, jnp.zeros((8, CHUNK), F32))
        lse = top + jnp.log2(jnp.sum(total, axis=0, keepdims=True))
        for k in range(CHUNK // 128):
            CV[0, pl.ds(xc * 4 + k, 1), 0] = lse[:, k * 128 : (k + 1) * 128]

    for k, d in enumerate((0,) + x_order):
        xc = (x + d) % XS
        if d:
            for e in range(ZS):
                arrived(xc * ZS + e)
            core_copy(xc, k).start()
        core_wait(xc, k)
        chunk_work(xc)

    def lse2(u, v):
        m = jnp.maximum(u, v)
        return m + jnp.log2(jnp.exp2(u - m) + jnp.exp2(v - m))

    def cp_copy(n):
        return copy(CV.at[n, pl.ds((1 - c) * 8, 8)], CP.at[n], cp_send.at[n], cp_recv.at[n], mate)

    def cx_copy(n, d):
        p = (idx + d) % CHIPS
        return copy(CX.at[n], CR.at[n, idx], cx_send.at[n, d], cx_recv.at[n, idx], chip(p))

    def cx_wait(n, d):
        p = (idx + d) % CHIPS
        copy(CX.at[n], CR.at[n, p], cx_send.at[n, d], cx_recv.at[n, p], chip(p)).wait_recv()

    def cf_copy(n):
        half = CF.at[n, pl.ds(c * 8, 8)]
        return copy(half, half, cf_send.at[n], cf_recv.at[n], mate)

    def column_exchange(n, log):
        cp_copy(n).start()
        cp_copy(n).wait_recv()
        mine = CV[n, pl.ds(c * 8, 8)]
        CX[n] = lse2(mine, CP[n]) if log else mine + CP[n]

        @pl.loop(1, CHIPS)
        def _(d):
            cx_copy(n, d).start()

        CR[n, pl.ds(idx, 1)] = CX[n][None]

        @pl.loop(1, CHIPS)
        def _(d):
            cx_wait(n, d)

        got = CR[n]
        if log:
            m = jnp.max(got, axis=0)
            half = m + jnp.log2(jnp.sum(jnp.exp2(got - m[None]), axis=0))
        else:
            half = jnp.sum(got, axis=0)
        CF[n, pl.ds(c * 8, 8)] = half
        cf_copy(n).start()
        cf_copy(n).wait_recv()

    column_exchange(0, True)
    for k in range(COLS // 128):
        GV[:, k * 128 : (k + 1) * 128] = math.log2(NS) - CF[0, k]

    eye = lax.broadcasted_iota(jnp.int32, (128, 128), 0) == lax.broadcasted_iota(
        jnp.int32, (128, 128), 1
    )

    def to_row(col):
        return jnp.sum(jnp.where(eye, col, 0.0), axis=0, keepdims=True)

    def to_col(row):
        return jnp.sum(jnp.where(eye, row, 0.0), axis=1, keepdims=True)

    def lanes(v):
        out = v[:, 0:128]
        for k in range(1, COLS // 128):
            out = out + v[:, k * 128 : (k + 1) * 128]
        return out

    STEP = 16

    def row_one(i, _):
        rows = pl.ds(pl.multiple_of(i * STEP, STEP), STEP)
        v = S[rows, :] + GV[...]
        top = jnp.max(v, axis=1, keepdims=True)
        e = jnp.exp2(v - top)
        S[rows, :] = e
        RB[rows, :] = lanes(e)
        TOPB[rows, :] = jnp.broadcast_to(top, (STEP, 128))
        return 0

    lax.fori_loop(0, ROWS // STEP, row_one, 0, unroll=2)

    def rr_copy(n, d):
        return copy(
            RV.at[n], RR.at[n, y], rr_send.at[n, d], rr_recv.at[n, y], {"tgt": (y + d) % YS}
        )

    def rr_wait(n, d):
        p = (y + d) % YS
        copy(RV.at[n], RR.at[n, p], rr_send.at[n, d], rr_recv.at[n, p], {"tgt": p}).wait_recv()

    def row_exchange(n):
        for d in range(1, YS):
            rr_copy(n, d).start()
        RR[n, pl.ds(y, 1)] = RV[n][None]
        for d in range(1, YS):
            rr_wait(n, d)
        return RR[n]

    for k in range(ROWS // 128):
        rows = pl.ds(k * 128, 128)
        total = jnp.sum(RB[rows, :], axis=1, keepdims=True)
        RV[0, k : k + 1] = to_row(TOPB[rows, :] + jnp.log2(total))
    got = row_exchange(0)
    m = jnp.max(got, axis=0)
    lse = m + jnp.log2(jnp.sum(jnp.exp2(got - m[None]), axis=0))
    FV[...] = math.log2(NT) - lse
    for k in range(ROWS // 128):
        rows = pl.ds(k * 128, 128)
        RB[rows, :] = jnp.exp2(TOPB[rows, :] + to_col(FV[k : k + 1, :]))

    def col_two(i, total):
        rows = pl.ds(pl.multiple_of(i * STEP, STEP), STEP)
        r = RB[rows, :]
        e = S[rows, :] * jnp.concatenate([r] * (COLS // 128), axis=1)
        S[rows, :] = e
        return total + e[0:8] + e[8:16]

    total = lax.fori_loop(0, ROWS // STEP, col_two, jnp.zeros((8, COLS), F32))
    total = jnp.sum(total, axis=0, keepdims=True)
    for k in range(COLS // 128):
        CV[1, k] = total[:, k * 128 : (k + 1) * 128]
    column_exchange(1, False)
    for k in range(COLS // 128):
        u = CF[1, k]
        g_ref[k] = (EPS * LN2) * (GV[:, k * 128 : (k + 1) * 128] + (math.log2(NS) - jnp.log2(u)))
        GV[:, k * 128 : (k + 1) * 128] = NS / u

    def row_two(i, _):
        rows = pl.ds(pl.multiple_of(i * STEP, STEP), STEP)
        e = S[rows, :] * GV[...]
        S[rows, :] = e
        RB[rows, :] = lanes(e)
        return 0

    lax.fori_loop(0, ROWS // STEP, row_two, 0)
    for k in range(ROWS // 128):
        rows = pl.ds(k * 128, 128)
        RV[1, k : k + 1] = to_row(jnp.sum(RB[rows, :], axis=1, keepdims=True))
    got = row_exchange(1)
    rho = (got[0] + got[1]) + (got[2] + got[3])
    f_ref[...] = (EPS * LN2) * (FV[...] + (math.log2(NT) - jnp.log2(rho)))
    FV[...] = NT / rho
    for k in range(ROWS // 128):
        rows = pl.ds(k * 128, 128)
        RB[rows, :] = jnp.broadcast_to(to_col(FV[k : k + 1, :]), (128, 128))

    MC = 256

    def rm_copy(k, d):
        p = (y + d) % YS
        cols = pl.ds(k * MC, MC)
        return copy(
            MT.at[pl.ds(pl.multiple_of(p * SLAB, 8), SLAB), cols], RM.at[d - 1, :, cols],
            rm_send.at[k, d], rm_recv.at[k, d], {"tgt": p},
        )

    for k in range(ROWS // MC):

        def weigh(i, _, k=k):
            rows = pl.ds(pl.multiple_of(k * MC + i * STEP, STEP), STEP)
            r = RB[rows, :]
            e = S[rows, :] * jnp.concatenate([r] * (COLS // 128), axis=1)
            W[pl.ds(pl.multiple_of(i * STEP, STEP), STEP), :] = e.astype(BF16)
            return 0

        lax.fori_loop(0, MC // STEP, weigh, 0)
        MT[:, k * MC : (k + 1) * MC] = dot(GT[...], W[...], NTD) * (1.0 / NT)
        for d in (2, 1, 3):
            rm_copy(k, d).start()

    grad = jnp.zeros((WIDE, D), F32)
    rest = MT[...]
    for part in range(3):
        piece = rest.astype(BF16)
        grad = grad + dot(piece, src_ref[...], NND)
        rest = rest - piece.astype(F32)
    GP[...] = jnp.zeros_like(GP)
    GP[:, 0:D] = grad * (EPS * math.sqrt(D) / NS)
    GB[...] = jnp.zeros_like(GB)
    for h in range(2):
        for t in range(3):
            GB[h, t * 20 : (t + 1) * 20] = GP[
                h * 160 : (h + 1) * 160, t * 128 : (t + 1) * 128
            ].reshape(20, 8, 128)

    gc = copy(GB.at[1 - c], GC, gc_send, gc_recv, mate)
    gc.start()
    gc.wait_recv()
    GS[...] = (GB[c] + GC[...]).reshape(CHIPS, 2, 8, 128)

    def gr_copy(d):
        p = (idx + d) % CHIPS
        return copy(GS.at[p], GR.at[idx], gr_send.at[d], gr_recv.at[idx], chip(p))

    def gr_wait(d):
        p = (idx + d) % CHIPS
        copy(GS.at[p], GR.at[p], gr_send.at[d], gr_recv.at[p], chip(p)).wait_recv()

    @pl.loop(1, CHIPS)
    def _(d):
        gr_copy(d).start()

    GR[pl.ds(idx, 1)] = GS[pl.ds(idx, 1)]

    @pl.loop(1, CHIPS)
    def _(d):
        gr_wait(d)

    GO[...] = jnp.sum(GR[...], axis=0)

    def gy_copy(d):
        return copy(GO, GY.at[y], gy_send.at[d], gy_recv.at[y], {"tgt": (y + d) % YS})

    def gy_wait(d):
        p = (y + d) % YS
        copy(GO, GY.at[p], gy_send.at[d], gy_recv.at[p], {"tgt": p}).wait_recv()

    for d in range(1, YS):
        gy_copy(d).start()
    GY[pl.ds(y, 1)] = GO[...][None]
    for d in range(1, YS):
        gy_wait(d)
    GZ[...] = (GY[0] + GY[1]) + (GY[2] + GY[3])

    def gz_copy(d):
        p = (idx + d) % CHIPS
        return copy(GZ, GF.at[c, idx], gz_send.at[d], gz_recv.at[idx], chip(p))

    def gz_wait(d):
        p = (idx + d) % CHIPS
        copy(GZ, GF.at[c, p], gz_send.at[d], gz_recv.at[p], chip(p)).wait_recv()

    @pl.loop(1, CHIPS)
    def _(d):
        gz_copy(d).start()

    GF[c, pl.ds(idx, 1)] = GZ[...][None]

    for k in range(ROWS // MC):
        for d in range(1, YS):
            rm_copy(k, d).wait_recv()
    own = MT[pl.ds(pl.multiple_of(y * SLAB, 8), SLAB), :]
    m_ref[...] = (own + RM[0]) + (RM[1] + RM[2])

    @pl.loop(1, CHIPS)
    def _(d):
        gz_wait(d)

    gf = copy(GF.at[c], GF.at[c], gf_send, gf_recv, mate)
    gf.start()
    gf.wait_recv()
    for h in range(2):
        flat = GF[h].reshape(TILES, 8, 128)
        for t in range(3):
            wide = min(128, D - t * 128)
            grad_ref[h * 160 : (h + 1) * 160, t * 128 : t * 128 + wide] = flat[
                t * 20 : (t + 1) * 20
            ].reshape(160, 128)[:, 0:wide]

    for d in z_order:
        z_copy(d).wait_send()
    for d in x_order:
        for k in range(ZS):
            x_copy(x * ZS + (z + k) % ZS, d, k).wait_send()
    for k, d in enumerate((0,) + x_order):
        core_copy((x + d) % XS, k).wait_send()
    for n in range(2):
        cp_copy(n).wait_send()
        cf_copy(n).wait_send()
        for d in range(1, YS):
            rr_copy(n, d).wait_send()
    for d in range(1, YS):
        gy_copy(d).wait_send()
        for k in range(ROWS // MC):
            rm_copy(k, d).wait_send()
    gc.wait_send()
    gf.wait_send()

    @pl.loop(1, CHIPS)
    def _(d):
        cx_copy(0, d).wait_send()
        cx_copy(1, d).wait_send()
        gr_copy(d).wait_send()
        gz_copy(d).wait_send()


def shards(source, target, rotation):
    vmem = pl.BlockSpec(memory_space=pltpu.VMEM)
    dma = pltpu.SemaphoreType.DMA
    scratch = [
        pltpu.VMEM((CHIPS, 2, 32, D), BF16),
        pltpu.VMEM((CHUNK, D), BF16),
        pltpu.VMEM((WIDE, COLS), BF16),
        pltpu.VMEM((ROWS, COLS), F32),
        pltpu.VMEM((256, COLS), BF16),
        pltpu.VMEM((WIDE, ROWS), F32),
        pltpu.VMEM((YS - 1, SLAB, ROWS), F32),
        pltpu.VMEM((ROWS, 128), F32),
        pltpu.VMEM((ROWS, 128), F32),
        pltpu.VMEM((2, 16, 1, 128), F32),
        pltpu.VMEM((2, 8, 1, 128), F32),
        pltpu.VMEM((2, 8, 1, 128), F32),
        pltpu.VMEM((2, CHIPS, 8, 1, 128), F32),
        pltpu.VMEM((2, 16, 1, 128), F32),
        pltpu.VMEM((1, COLS), F32),
        pltpu.VMEM((2, 8, 128), F32),
        pltpu.VMEM((2, YS, 8, 128), F32),
        pltpu.VMEM((8, 128), F32),
        pltpu.VMEM((WIDE, 384), F32),
        pltpu.VMEM((2, TILES, 8, 128), F32),
        pltpu.VMEM((TILES, 8, 128), F32),
        pltpu.VMEM((CHIPS, 2, 8, 128), F32),
        pltpu.VMEM((CHIPS, 2, 8, 128), F32),
        pltpu.VMEM((2, 8, 128), F32),
        pltpu.VMEM((YS, 2, 8, 128), F32),
        pltpu.VMEM((2, 8, 128), F32),
        pltpu.VMEM((2, CHIPS, 2, 8, 128), F32),
        dma((ZS,)), dma((CHIPS, 2)), dma((XS, ZS)), dma((XS,)),
        dma((2,)), dma((2,)), dma((2, CHIPS)), dma((2, CHIPS)), dma((2,)), dma((2,)),
        dma((2, YS)), dma((2, YS)), dma((4, YS)), dma((4, YS)),
        dma, dma, dma((CHIPS,)), dma((CHIPS,)), dma((YS,)), dma((YS,)),
        dma((CHIPS,)), dma((CHIPS,)), dma, dma,
    ]
    f, g, m, grad = pl.pallas_call(
        kernel,
        out_shape=(
            jax.ShapeDtypeStruct((8, 128), F32),
            jax.ShapeDtypeStruct((16, 1, 128), F32),
            jax.ShapeDtypeStruct((SLAB, ROWS), F32),
            jax.ShapeDtypeStruct((WIDE, D), F32),
        ),
        in_specs=[vmem] * 3,
        out_specs=(vmem,) * 4,
        scratch_shapes=scratch,
        compiler_params=pltpu.CompilerParams(
            collective_id=0, has_side_effects=True, vmem_limit_bytes=48 << 20
        ),
        name="sinkhorn_step",
    )(source, target, rotation)
    rotation_grad = grad.reshape(YS, SLAB, D)[:, :75].reshape(D, D).T
    return (f.reshape(ROWS), g.reshape(COLS), m[:75].T, rotation_grad)


def solution(mesh):
    placed = (P("src", None), P(("tgt", "src"), None), P())
    return jax.shard_map(
        shards,
        mesh=mesh,
        in_specs=placed,
        out_specs=(P("src"), P("tgt"), P("src", "tgt"), P()),
        check_vma=False,
    )
```

time: 929 us -> 109 us (0.12)
  blocking collectives: 538 us -> 0 us
  waiting for transfers between devices: 313 us -> 0 us
  Pallas kernels: 0 us -> 104 us
  matrix products: 49.1 us -> 0 us
  between operations: 14 us -> 0.68 us
    pmax x4 -> x0, blocking collectives: 272 us -> none  [the longest x2 256 us: shards(): peak = lax.pmax(tops, 'src')]
    psum x4 -> x0, blocking collectives: 267 us -> none  [the longest x2 255 us: shards(): totals = lax.psum(totals * jnp.exp(tops - peak), 'src')]
    psum x2 -> x0, waiting for transfers between devices: 228 us -> none  [the longest x1 180 us: shards(): rotation_grad = lax.psum(partial_grad, 'src')]
    pallas_call x0 -> x1, Pallas kernels: none -> 104 us  [shards(): pl.pallas_call(kernel, out_shape=(jax.ShapeDtypeStruct((8, 128), F32), ja...]
    all_gather x1 -> x0, waiting for transfers between devices: 83.9 us -> none  [shards(): targets_all = lax.all_gather(target, 'src', axis=0, tiled=True)]
    dot_general x22 -> x0, matrix products: 49.1 us -> none  [the longest x16 28.2 us: cost_block(): jnp.einsum('rd,cd->rc', source, piece, preferred_element_type=jnp.float32)]
  transfers between devices with their start and end apart: 3 -> 0, of which waited for: 3 -> 0; matrix products, arithmetic and copies ran while one was open for 0% -> 0% of each run, Pallas kernels for 0% -> 0%
where the time goes in v1:
time: 109 us
  Pallas kernels  104 us (95%)
  local copies, waits for them, and re-layouts  4.47 us (4%)
    pallas_call x1, Pallas kernels, shards(): pl.pallas_call(kernel, out_shape=(jax.ShapeDtypeStruct((8, 128), F32), ja...  104 us
    unnamed x8, local copies, waits for them, and re-layouts  3.67 us

profile of v1, /device:TPU:1, one launch (start us, length us, event | category | flops | bytes accessed | tf_op | source)
XLA Modules:
  0.0 108.8 jit_solution(7770156937349319854)
XLA Ops:
  0.6 0.0 copy-start
  0.6 0.0 copy-start.1
  0.7 1.5 %copy.9.src_ref = bf16[1024,300]{1,0:T(8,128)(2,1)S(1)} copy(bf16[1024,300]{0,1:T(8,128)(2,1)} %param.3) | data formatting | bytes 1228800 | tf_op args[0]
  2.1 0.0 copy-done
  2.1 0.0 copy-done.1
  2.2 103.6 %sinkhorn_step.1 = (f32[8,128]{1,0:T(8,128)S(1)}, f32[16,1,128]{2,1,0:T(1,128)S(1)}, f32[80,1024]{1,0:T(8,128)S(1)}, f32[320,300]{1,0:T(8,128)S(1)}) custom-call(bf16[1024,300]{1,0:T(8,128)(2,1)S(1)} %copy.9.src_ref, bf16[32,300]{1,0:T(8,128)(2,1)S(1)} %copy-done.1, bf16[300,300]{1,0:T(8,128)(2,1)S(1)} %copy-done), custom_call_target="tpu_custom_call" | custom-call | tf_op jit(solution)/shard_map/sinkhorn_step/pallas_call | solution.py:478
  105.8 0.7 slice_bitcast_fusion
  106.5 0.1 reshape.23
  106.6 1.0 copy.10
  107.6 0.6 copy.13
  108.2 0.6 copy.14
Async XLA Ops:
  0.6 1.5 %copy-start = (bf16[300,300]{1,0:T(8,128)(2,1)S(1)}, bf16[300,300]{1,0:T(8,128)(2,1)}, u32[]{:S(2)}) copy-start(bf16[300,300]{1,0:T(8,128)(2,1)} %rot_ref.1) | copy-start | bytes 540004
  0.6 1.5 %copy-start.1 = (bf16[32,300]{1,0:T(8,128)(2,1)S(1)}, bf16[32,300]{1,0:T(8,128)(2,1)}, u32[]{:S(2)}) copy-start(bf16[32,300]{1,0:T(8,128)(2,1)} %tgt_ref.1) | copy-start | bytes 57604

commit v2 on v1

v2 whole, which is shorter than its diff:
```python
import functools
import math

import jax
import jax.numpy as jnp
from jax import lax
from jax.experimental import pallas as pl
from jax.experimental.pallas import tpu as pltpu
from jax.sharding import PartitionSpec as P

MESH = pl.DeviceIdType.MESH
F32 = jnp.float32
BF16 = jnp.bfloat16

XS, ZS, YS = 4, 8, 4
CHIPS = XS * ZS
D = 300
ROWS = 1024
COLS = 2048
NS, NT = 65536, 8192
EPS = 2.0
LN2 = math.log(2.0)
SLAB = 80
WIDE = YS * SLAB
CHUNK = 512
RT8 = 19
TILES = 64
NTD = (((1,), (1,)), ((), ()))
NND = (((1,), (0,)), ((), ()))


def hops(d):
    return min(d // ZS, XS - d // ZS) + min(d % ZS, ZS - d % ZS)


FAR = sorted(range(1, CHIPS), key=hops, reverse=True)


def dot(a, b, dims):
    return lax.dot_general(a, b, dims, preferred_element_type=F32)


def kernel(
    src_hbm, tgt_hbm, rot_hbm,
    f_ref, g_ref, m_ref, grad_ref,
    G, ST, SRC, RQ, RT, GT, S, W, MT, RM, TOPB, RB,
    CV, CP, CX, CR, CF, GV,
    RV, RR, FV,
    GP, GB, GC, GS, GR, GO, GY, GZ, GF,
    load, gather_send, gather_recv, fwd_send, core_send, block_send,
    cp_send, cp_recv, cx_send, cx_recv, cf_send, cf_recv,
    rr_send, rr_recv, rm_send, rm_recv,
    gc_send, gc_recv, gr_send, gr_recv, gy_send, gy_recv, gz_send, gz_recv, gf_send, gf_recv,
):
    s = lax.axis_index("src")
    y = lax.axis_index("tgt")
    idx = s // 2
    c = s % 2
    x = idx // ZS
    z = idx % ZS
    mate = {"src": idx * 2 + (1 - c)}

    def chip(p):
        return {"src": p * 2 + c}

    def copy(a, b, ss, rs, to):
        return pltpu.make_async_remote_copy(
            src_ref=a, dst_ref=b, send_sem=ss, recv_sem=rs, device_id=to, device_id_type=MESH
        )

    loads = (
        pltpu.make_async_copy(tgt_hbm, G.at[idx, c], load.at[0]),
        pltpu.make_async_copy(rot_hbm, RQ, load.at[1]),
        pltpu.make_async_copy(src_hbm, ST, load.at[2]),
    )
    for one in loads:
        one.start()

    barrier = pltpu.get_barrier_semaphore()

    for d in (4, 3, 5, 2, 6, 1, 7):
        to = chip(x * ZS + (z + d) % ZS)
        pl.semaphore_signal(barrier, inc=1, device_id=to, device_id_type=MESH)
    for d in (2, 1, 3):
        to = chip(((x + d) % XS) * ZS + z)
        pl.semaphore_signal(barrier, inc=1, device_id=to, device_id_type=MESH)
        pl.semaphore_signal(barrier, inc=1, device_id={"tgt": (y + d) % YS}, device_id_type=MESH)
    pl.semaphore_signal(barrier, inc=1, device_id=mate, device_id_type=MESH)
    pl.semaphore_wait(barrier, ZS - 1 + XS - 1 + YS - 1 + 1)

    def z_copy(d):
        return copy(
            G.at[idx, c], G.at[idx, c], gather_send.at[d], gather_recv.at[idx, c],
            chip(x * ZS + (z + d) % ZS),
        )

    def x_copy(p, d, k):
        return copy(
            G.at[p, c], G.at[p, c], fwd_send.at[d, k], gather_recv.at[p, c],
            chip(((x + d) % XS) * ZS + z),
        )

    def core_copy(xc, k):
        block = G.at[pl.ds(xc * ZS, ZS), c]
        return copy(block, block, core_send.at[k], gather_recv.at[xc * ZS, c], mate)

    def block_copy(p, d):
        return copy(G.at[p, c], G.at[p, c], block_send.at[d], gather_recv.at[p, c], mate)

    def block_wait(p):
        other = G.at[p, 1 - c]
        copy(other, other, block_send.at[0], gather_recv.at[p, 1 - c], mate).wait_recv()

    def core_wait(xc, k):
        block = G.at[pl.ds(xc * ZS, ZS), 1 - c]
        copy(block, block, core_send.at[k], gather_recv.at[xc * ZS, 1 - c], mate).wait_recv()

    def arrived(p):
        copy(
            G.at[p, c], G.at[p, c], gather_send.at[0], gather_recv.at[p, c], mate
        ).wait_recv()

    z_order = (1, 7, 2, 6, 3, 5, 4)
    x_order = (1, 3, 2)
    loads[0].wait()
    for d in z_order:
        z_copy(d).start()
    for d in x_order:
        x_copy(idx, d, 0).start()
    block_copy(idx, 0).start()
    loads[1].wait()
    loads[2].wait()
    SRC[...] = ST[...].T
    a = lax.broadcasted_iota(jnp.int32, (WIDE, D), 0)
    b = lax.broadcasted_iota(jnp.int32, (WIDE, D), 1)
    hit = jnp.zeros((WIDE, D), jnp.bool_)
    for q in range(YS):
        hit = hit | ((a - SLAB * q == b - 75 * q) & (b >= 75 * q) & (b < 75 * q + 75))
    spread = jnp.where(hit, 1.0, 0.0).astype(BF16)

    for d in z_order:
        p = x * ZS + (z + d) % ZS
        arrived(p)
        for e in x_order:
            x_copy(p, e, d).start()
        block_copy(p, d).start()

    scale = math.log2(math.e) / (EPS * math.sqrt(D))
    HALF = 256

    def chunk_work(xc):
        words = G[pl.ds(xc * ZS, ZS)].reshape(CHUNK, D)
        GT[:, pl.ds(pl.multiple_of(xc * CHUNK, CHUNK), CHUNK)] = dot(spread, words, NTD).astype(BF16)
        RT[...] = dot(RQ[...], words, NTD).astype(BF16)
        for h in range(CHUNK // HALF):
            cols = pl.ds(pl.multiple_of(xc * CHUNK + h * HALF, HALF), HALF)
            part = dot(SRC[...], RT[:, h * HALF : (h + 1) * HALF], NND) * scale
            S[:, cols] = part
            top = jnp.max(part, axis=0, keepdims=True)
            total = jnp.sum(jnp.exp2(S[:, cols] - top), axis=0, keepdims=True)
            lse = top + jnp.log2(total)
            for k in range(HALF // 128):
                CV[0, pl.ds(xc * 4 + h * 2 + k, 1), 0] = lse[:, k * 128 : (k + 1) * 128]

    def forward(d):
        xc = (x + d) % XS
        for e in range(ZS):
            arrived(xc * ZS + e)
        core_copy(xc, d).start()

    def finish(d):
        xc = (x + d) % XS
        core_wait(xc, d)
        chunk_work(xc)

    for e in range(ZS):
        block_wait(x * ZS + e)
    chunk_work(x)
    forward(1)
    forward(3)
    finish(1)
    forward(2)
    finish(3)
    finish(2)

    def lse2(u, v):
        m = jnp.maximum(u, v)
        return m + jnp.log2(jnp.exp2(u - m) + jnp.exp2(v - m))

    def cp_copy(n):
        return copy(CV.at[n, pl.ds((1 - c) * 8, 8)], CP.at[n], cp_send.at[n], cp_recv.at[n], mate)

    def cx_copy(n, d):
        p = ((x + d // ZS) % XS) * ZS + (z + d % ZS) % ZS
        return copy(CX.at[n], CR.at[n, idx], cx_send.at[n, d], cx_recv.at[n, idx], chip(p))

    def cx_wait(n, d):
        p = ((x + d // ZS) % XS) * ZS + (z + d % ZS) % ZS
        copy(CX.at[n], CR.at[n, p], cx_send.at[n, d], cx_recv.at[n, p], chip(p)).wait_recv()

    def cf_copy(n):
        half = CF.at[n, pl.ds(c * 8, 8)]
        return copy(half, half, cf_send.at[n], cf_recv.at[n], mate)

    def column_exchange(n, log):
        cp_copy(n).start()
        cp_copy(n).wait_recv()
        mine = CV[n, pl.ds(c * 8, 8)]
        CX[n] = lse2(mine, CP[n]) if log else mine + CP[n]

        for d in FAR:
            cx_copy(n, d).start()

        CR[n, pl.ds(idx, 1)] = CX[n][None]

        for d in FAR[::-1]:
            cx_wait(n, d)

        got = CR[n]
        if log:
            m = jnp.max(got, axis=0)
            half = m + jnp.log2(jnp.sum(jnp.exp2(got - m[None]), axis=0))
        else:
            half = jnp.sum(got, axis=0)
        CF[n, pl.ds(c * 8, 8)] = half
        cf_copy(n).start()
        cf_copy(n).wait_recv()

    column_exchange(0, True)
    for k in range(COLS // 128):
        GV[:, k * 128 : (k + 1) * 128] = math.log2(NS) - CF[0, k]

    eye = lax.broadcasted_iota(jnp.int32, (128, 128), 0) == lax.broadcasted_iota(
        jnp.int32, (128, 128), 1
    )

    def to_row(col):
        return jnp.sum(jnp.where(eye, col, 0.0), axis=0, keepdims=True)

    def to_col(row):
        return jnp.sum(jnp.where(eye, row, 0.0), axis=1, keepdims=True)

    STEP = 16
    BLOCK = 128

    def row_one(i, _):
        rows = pl.ds(pl.multiple_of(i * BLOCK, BLOCK), BLOCK)
        top = S[rows, 0:128] + GV[:, 0:128]
        for k in range(1, COLS // 128):
            cols = slice(k * 128, (k + 1) * 128)
            top = jnp.maximum(top, S[rows, cols] + GV[:, cols])
        top = jnp.broadcast_to(jnp.max(top, axis=1, keepdims=True), (BLOCK, 128))
        TOPB[rows, :] = top
        total = jnp.zeros((BLOCK, 128), F32)
        for k in range(COLS // 128):
            cols = slice(k * 128, (k + 1) * 128)
            e = jnp.exp2((S[rows, cols] + GV[:, cols]) - top)
            S[rows, cols] = e
            total = total + e
        total = jnp.sum(total, axis=1, keepdims=True)
        RV[0, pl.ds(i, 1), 0] = to_row(top + jnp.log2(total))
        return 0

    lax.fori_loop(0, ROWS // BLOCK, row_one, 0)

    def rr_copy(n, d):
        return copy(
            RV.at[n], RR.at[n, y], rr_send.at[n, d], rr_recv.at[n, y], {"tgt": (y + d) % YS}
        )

    def rr_wait(n, d):
        p = (y + d) % YS
        copy(RV.at[n], RR.at[n, p], rr_send.at[n, d], rr_recv.at[n, p], {"tgt": p}).wait_recv()

    def row_exchange(n):
        for d in range(1, YS):
            rr_copy(n, d).start()
        RR[n, pl.ds(y, 1)] = RV[n][None]
        for d in range(1, YS):
            rr_wait(n, d)
        return RR[n]

    got = row_exchange(0)
    m = jnp.max(got, axis=0)
    lse = m + jnp.log2(jnp.sum(jnp.exp2(got - m[None]), axis=0))
    FV[...] = math.log2(NT) - lse
    for k in range(ROWS // 128):
        rows = pl.ds(k * 128, 128)
        RB[rows, :] = jnp.exp2(TOPB[rows, :] + to_col(FV[k]))

    def col_two(i, total):
        rows = pl.ds(pl.multiple_of(i * STEP, STEP), STEP)
        r = RB[rows, :]
        e = S[rows, :] * jnp.concatenate([r] * (COLS // 128), axis=1)
        S[rows, :] = e
        return total + e[0:8] + e[8:16]

    total = lax.fori_loop(0, ROWS // STEP, col_two, jnp.zeros((8, COLS), F32))
    total = jnp.sum(total, axis=0, keepdims=True)
    for k in range(COLS // 128):
        CV[1, k] = total[:, k * 128 : (k + 1) * 128]
    column_exchange(1, False)
    for k in range(COLS // 128):
        u = CF[1, k]
        g_ref[k] = (EPS * LN2) * (GV[:, k * 128 : (k + 1) * 128] + (math.log2(NS) - jnp.log2(u)))
        GV[:, k * 128 : (k + 1) * 128] = NS / u

    def row_two(i, _):
        rows = pl.ds(pl.multiple_of(i * BLOCK, BLOCK), BLOCK)
        total = jnp.zeros((BLOCK, 128), F32)
        for k in range(COLS // 128):
            cols = slice(k * 128, (k + 1) * 128)
            e = S[rows, cols] * GV[:, cols]
            S[rows, cols] = e
            total = total + e
        RV[1, pl.ds(i, 1), 0] = to_row(jnp.sum(total, axis=1, keepdims=True))
        return 0

    lax.fori_loop(0, ROWS // BLOCK, row_two, 0)
    got = row_exchange(1)
    rho = (got[0] + got[1]) + (got[2] + got[3])
    f_ref[...] = (EPS * LN2) * (FV[...] + (math.log2(NT) - jnp.log2(rho)))
    FV[...] = NT / rho
    for k in range(ROWS // 128):
        rows = pl.ds(k * 128, 128)
        RB[rows, :] = jnp.broadcast_to(to_col(FV[k]), (128, 128))

    MC = 256

    def rm_copy(k, d):
        p = (y + d) % YS
        return copy(
            MT.at[k, p], RM.at[d - 1, k],
            rm_send.at[k, d], rm_recv.at[k, d], {"tgt": p},
        )

    for k in range(ROWS // MC):

        def weigh(i, _, k=k):
            rows = pl.ds(pl.multiple_of(k * MC + i * STEP, STEP), STEP)
            r = RB[rows, :]
            e = S[rows, :] * jnp.concatenate([r] * (COLS // 128), axis=1)
            W[pl.ds(pl.multiple_of(i * STEP, STEP), STEP), :] = e.astype(BF16)
            return 0

        lax.fori_loop(0, MC // STEP, weigh, 0)
        part = dot(GT[...], W[...], NTD) * (1.0 / NT)
        MT[k] = part.reshape(YS, SLAB, MC)
        for d in (2, 1, 3):
            rm_copy(k, d).start()

    grad = jnp.zeros((D, WIDE), F32)
    for k in range(ROWS // MC):
        rest = MT[k].reshape(WIDE, MC)
        for part in range(3):
            piece = rest.astype(BF16)
            grad = grad + dot(ST[:, k * MC : (k + 1) * MC], piece, NTD)
            rest = rest - piece.astype(F32)
    GP[...] = jnp.zeros_like(GP)
    GP[0:D, 0:WIDE] = grad * (EPS * math.sqrt(D) / NS)
    GB[:, 3 * RT8 :] = jnp.zeros((2, TILES - 3 * RT8, 8, 128), F32)
    for h in range(2):
        for t in range(3):
            GB[h, t * RT8 : (t + 1) * RT8] = GP[
                h * RT8 * 8 : (h + 1) * RT8 * 8, t * 128 : (t + 1) * 128
            ].reshape(RT8, 8, 128)

    gc = copy(GB.at[1 - c], GC, gc_send, gc_recv, mate)
    gc.start()
    gc.wait_recv()
    GS[...] = (GB[c] + GC[...]).reshape(CHIPS, 2, 8, 128)

    def gr_copy(d):
        p = ((x + d // ZS) % XS) * ZS + (z + d % ZS) % ZS
        return copy(GS.at[p], GR.at[idx], gr_send.at[d], gr_recv.at[idx], chip(p))

    def gr_wait(d):
        p = ((x + d // ZS) % XS) * ZS + (z + d % ZS) % ZS
        copy(GS.at[p], GR.at[p], gr_send.at[d], gr_recv.at[p], chip(p)).wait_recv()

    for d in FAR:
        gr_copy(d).start()

    GR[pl.ds(idx, 1)] = GS[pl.ds(idx, 1)]

    for d in FAR[::-1]:
        gr_wait(d)

    GO[...] = jnp.sum(GR[...], axis=0)

    def gy_copy(d):
        return copy(GO, GY.at[y], gy_send.at[d], gy_recv.at[y], {"tgt": (y + d) % YS})

    def gy_wait(d):
        p = (y + d) % YS
        copy(GO, GY.at[p], gy_send.at[d], gy_recv.at[p], {"tgt": p}).wait_recv()

    for d in range(1, YS):
        gy_copy(d).start()
    GY[pl.ds(y, 1)] = GO[...][None]
    for d in range(1, YS):
        gy_wait(d)
    GZ[...] = (GY[0] + GY[1]) + (GY[2] + GY[3])

    def gz_copy(d):
        p = ((x + d // ZS) % XS) * ZS + (z + d % ZS) % ZS
        return copy(GZ, GF.at[c, idx], gz_send.at[d], gz_recv.at[idx], chip(p))

    def gz_wait(d):
        p = ((x + d // ZS) % XS) * ZS + (z + d % ZS) % ZS
        copy(GZ, GF.at[c, p], gz_send.at[d], gz_recv.at[p], chip(p)).wait_recv()

    for d in FAR:
        gz_copy(d).start()

    GF[c, pl.ds(idx, 1)] = GZ[...][None]

    for k in range(ROWS // MC):
        for d in range(1, YS):
            rm_copy(k, d).wait_recv()
    for k in range(ROWS // MC):
        m_ref[:, k * MC : (k + 1) * MC] = (
            (MT[k, y] + RM[0, k]) + (RM[1, k] + RM[2, k])
        )[0:75]

    for d in FAR[::-1]:
        gz_wait(d)

    gf = copy(GF.at[c], GF.at[c], gf_send, gf_recv, mate)
    gf.start()
    gf.wait_recv()
    for h in range(2):
        flat = GF[h].reshape(TILES, 8, 128)
        for t in range(3):
            GP[h * RT8 * 8 : (h + 1) * RT8 * 8, t * 128 : (t + 1) * 128] = flat[
                t * RT8 : (t + 1) * RT8
            ].reshape(RT8 * 8, 128)
    for q in range(YS):
        grad_ref[:, q * 75 : (q + 1) * 75] = GP[0:D, q * SLAB : q * SLAB + 75]

    for d in z_order:
        z_copy(d).wait_send()
    for d in x_order:
        for k in range(ZS):
            x_copy(x * ZS + (z + k) % ZS, d, k).wait_send()
        core_copy((x + d) % XS, d).wait_send()
    for d in range(ZS):
        block_copy(x * ZS + (z + d) % ZS, d).wait_send()
    for n in range(2):
        cp_copy(n).wait_send()
        cf_copy(n).wait_send()
        for d in range(1, YS):
            rr_copy(n, d).wait_send()
    for d in range(1, YS):
        gy_copy(d).wait_send()
        for k in range(ROWS // MC):
            rm_copy(k, d).wait_send()
    gc.wait_send()
    gf.wait_send()

    for d in FAR:
        cx_copy(0, d).wait_send()
        cx_copy(1, d).wait_send()
        gr_copy(d).wait_send()
        gz_copy(d).wait_send()


def emit(*refs):
    sems = refs[8]
    copies = [pltpu.make_async_copy(refs[i], refs[4 + i], sems.at[i]) for i in range(4)]
    for one in copies:
        one.start()
    for one in copies:
        one.wait()


def shards(source, target, rotation):
    vmem = pl.BlockSpec(memory_space=pltpu.VMEM)
    dma = pltpu.SemaphoreType.DMA
    scratch = [
        pltpu.VMEM((CHIPS, 2, 32, D), BF16),
        pltpu.VMEM((D, ROWS), BF16),
        pltpu.VMEM((ROWS, D), BF16),
        pltpu.VMEM((D, D), BF16),
        pltpu.VMEM((D, CHUNK), BF16),
        pltpu.VMEM((WIDE, COLS), BF16),
        pltpu.VMEM((ROWS, COLS), F32),
        pltpu.VMEM((256, COLS), BF16),
        pltpu.VMEM((4, YS, SLAB, 256), F32),
        pltpu.VMEM((YS - 1, 4, SLAB, 256), F32),
        pltpu.VMEM((ROWS, 128), F32),
        pltpu.VMEM((ROWS, 128), F32),
        pltpu.VMEM((2, 16, 1, 128), F32),
        pltpu.VMEM((2, 8, 1, 128), F32),
        pltpu.VMEM((2, 8, 1, 128), F32),
        pltpu.VMEM((2, CHIPS, 8, 1, 128), F32),
        pltpu.VMEM((2, 16, 1, 128), F32),
        pltpu.VMEM((1, COLS), F32),
        pltpu.VMEM((2, 8, 1, 128), F32),
        pltpu.VMEM((2, YS, 8, 1, 128), F32),
        pltpu.VMEM((8, 1, 128), F32),
        pltpu.VMEM((2 * RT8 * 8, 384), F32),
        pltpu.VMEM((2, TILES, 8, 128), F32),
        pltpu.VMEM((TILES, 8, 128), F32),
        pltpu.VMEM((CHIPS, 2, 8, 128), F32),
        pltpu.VMEM((CHIPS, 2, 8, 128), F32),
        pltpu.VMEM((2, 8, 128), F32),
        pltpu.VMEM((YS, 2, 8, 128), F32),
        pltpu.VMEM((2, 8, 128), F32),
        pltpu.VMEM((2, CHIPS, 2, 8, 128), F32),
        dma((3,)), dma((ZS,)), dma((CHIPS, 2)), dma((XS, ZS)), dma((XS,)), dma((ZS,)),
        dma((2,)), dma((2,)), dma((2, CHIPS)), dma((2, CHIPS)), dma((2,)), dma((2,)),
        dma((2, YS)), dma((2, YS)), dma((4, YS)), dma((4, YS)),
        dma, dma, dma((CHIPS,)), dma((CHIPS,)), dma((YS,)), dma((YS,)),
        dma((CHIPS,)), dma((CHIPS,)), dma, dma,
    ]
    f, g, m, grad = pl.pallas_call(
        kernel,
        out_shape=(
            jax.ShapeDtypeStruct((8, 1, 128), F32),
            jax.ShapeDtypeStruct((16, 1, 128), F32),
            jax.ShapeDtypeStruct((75, ROWS), F32),
            jax.ShapeDtypeStruct((D, D), F32),
        ),
        in_specs=[pl.BlockSpec(memory_space=pltpu.HBM)] * 3,
        out_specs=(vmem,) * 4,
        scratch_shapes=scratch,
        compiler_params=pltpu.CompilerParams(
            collective_id=0, has_side_effects=True, vmem_limit_bytes=63 << 20
        ),
        name="sinkhorn_step",
    )(source.T, target, rotation)
    f, g, m, grad = pl.pallas_call(
        emit,
        out_shape=tuple(jax.ShapeDtypeStruct(a.shape, a.dtype) for a in (f, g, m, grad)),
        in_specs=[vmem] * 4,
        out_specs=(pl.BlockSpec(memory_space=pl.ANY),) * 4,
        scratch_shapes=[dma((4,))],
        name="write_results",
    )(f, g, m, grad)
    return (f.reshape(ROWS), g.reshape(COLS), m.T, grad)


def solution(mesh):
    placed = (P("src", None), P(("tgt", "src"), None), P())
    return jax.shard_map(
        shards,
        mesh=mesh,
        in_specs=placed,
        out_specs=(P("src"), P("tgt"), P("src", "tgt"), P()),
        check_vma=False,
    )
```

time: 109 us -> 93.7 us (0.86)
  Pallas kernels: 104 us -> 92.8 us
  local copies, waits for them, and re-layouts: 4.47 us -> 0 us
    pallas_call x1 -> x2, Pallas kernels: 104 us -> 92.8 us  [the longest x1 90.7 us: shards(): pl.pallas_call(kernel, out_shape=(jax.ShapeDtypeStruct((8, 1, 128), F32),...]
    unnamed x8 -> x0, local copies, waits for them, and re-layouts: 3.67 us -> none
where the time goes in v2:
time: 93.7 us; the launch traced here: 93.6 us
  Pallas kernels  92.8 us (99%)
    pallas_call x1, Pallas kernels, shards(): pl.pallas_call(kernel, out_shape=(jax.ShapeDtypeStruct((8, 1, 128), F32),...  90.7 us
    pallas_call x1, Pallas kernels, shards(): pl.pallas_call(emit, out_shape=tuple((jax.ShapeDtypeStruct(a.shape, a.dty...  2.06 us

profile of v2, /device:TPU:1, one launch (start us, length us, event | category | flops | bytes accessed | tf_op | source)
XLA Modules:
  0.0 93.6 jit_solution(16684711891433187102)
XLA Ops:
  0.6 90.7 %sinkhorn_step.1 = (f32[8,1,128]{2,1,0:T(1,128)}, f32[16,1,128]{2,1,0:T(1,128)}, f32[75,1024]{1,0:T(8,128)}, f32[300,300]{1,0:T(8,128)}) custom-call(bf16[300,1024]{1,0:T(8,128)(2,1)} %bitcast.4, bf16[32,300]{1,0:T(8,128)(2,1)} %tgt_hbm.1, bf16[300,300]{1,0:T(8,128)(2,1)} %rot_hbm.1), custom_call_target="tpu_custom_call" | custom-call | tf_op jit(solution)/shard_map/sinkhorn_step/pallas_call | solution.py:517
  91.4 2.1 %write_results.1 = (f32[8,1,128]{2,1,0:T(1,128)}, f32[16,1,128]{2,1,0:T(1,128)}, f32[75,1024]{1,0:T(8,128)}, f32[300,300]{1,0:T(8,128)}) custom-call(f32[8,1,128]{2,1,0:T(1,128)} %get-tuple-element.12.refs_0_, f32[16,1,128]{2,1,0:T(1,128)} %get-tuple-element.13.refs_1_, f32[75,1024]{1,0:T(8,128)} %get-tuple-element.14.refs_2_, ...), custom_call_target="tpu_custom_call" | custom-call | tf_op jit(solution)/shard_map/write_results/pallas_call | solution.py:533
